TPU v7x, 256 devices: a whole 4x4x8 slice. The times are simulated.
256 devices in a mesh: stream: 32 (over y, z_lo, x), span: 8 (over z_hi, core).
Axes of the slice: x: 4, y: 4, z: 8 (z_hi: 4, z_lo: 2; z = z_hi * 2 + z_lo), core: 2. Of those that a mesh axis runs over, the one named last changes fastest.
Arguments:
- adjoint_start: float32 [5, 256, 128, 512], P(None, 'stream', 'span'), may hold values from -4 to 4
- source: float32 [5, 256, 128, 512], P(None, 'stream', 'span'), may hold values from -40 to 40
- flow_state: float32 [5, 256, 128, 512], P(None, 'stream', 'span'), may hold values from -4 to 4, as said below
- precond: float32 [5, 5, 256, 128, 512], P(None, None, 'stream', 'span'), may hold values from -0.12 to 0.2
- flux_jac: float32 [3, 5, 5], replicated, may hold values from -4 to 4
- bc_codes: int32 [256, 128], P('stream', 'span'), may hold values from 0 to 2
Outputs:
- adjoint: float32 [5, 256, 128, 512], P(None, 'stream', 'span')
- residual_rms: float32 [2], replicated
Inputs may be any that keep to these rules, and one draw needn't show every extreme that they name: `bc_codes`: 0 is a wall, 1 a far field, 2 an extrapolation face. `flow_state`: density and pressure lie in 0.5 to 2.
All inputs are finite; a program needn't handle non-finite values.
Results may differ from a plain program's by a relative error of at most 0.0003.
Values sent between devices are 32-bit elements; how exact they have to be, the bound alone decides.
A program may use at most 128 MiB of HBM per device.

v0:
```python
import functools

import jax
import jax.numpy as jnp
from jax import lax
from jax.experimental import pallas as pl
from jax.experimental.pallas import tpu as pltpu
from jax.sharding import PartitionSpec as P

MESH = pl.DeviceIdType.MESH
NV = 5
J0 = 8


def ring(value, step, size):
    return lax.rem(value + step, size)


def reduction_partners(stream, span):
    y, z_lo, x = stream // 8, lax.rem(stream // 4, 2), lax.rem(stream, 4)
    z_hi, core = span // 2, lax.rem(span, 2)

    def at(dy, dl, dx, dh, dc):
        line = ring(y, dy, 4) * 8 + ring(z_lo, dl, 2) * 4 + ring(x, dx, 4)
        return (line, ring(z_hi, dh, 4) * 2 + ring(core, dc, 2))

    far = (2, 1, 3, 0)
    first = [(0, dl, 0, dh, dc) for dh in far for dl in (1, 0) for dc in (1, 0)]
    order = sorted(((dy, dx) for dy in range(4) for dx in range(4)), key=lambda d: -sum(min(t, 4 - t) for t in d))
    second = [(dy, 0, dx, 0, 0) for dy, dx in order]
    return [[at(*step) for step in steps if any(step)] for steps in (first, second)]


def kernel(
    cells_all, start_ref, source_ref, flow_ref, precond_ref, jac_ref, codes_ref, out, rms_ref,
    v0, v1, speed, flow, source, precond, jac, codes, ghost, flip, part, gathered,
    load_sem, i_send, i_recv, j_send, j_recv, s_send, s_recv, r_send, r_recv,
):
    stream, span = lax.axis_index("stream"), lax.axis_index("span")
    streams, spans = lax.axis_size("stream"), lax.axis_size("span")
    ni, nj, nk = flow.shape[1:]
    chunks = nk // 128
    rows = pl.ds(J0, nj)

    i_side = [(stream > 0, (stream - 1, span)), (stream < streams - 1, (stream + 1, span))]
    j_side = [(span > 0, (stream, span - 1)), (span < spans - 1, (stream, span + 1))]
    stages = reduction_partners(stream, span)

    barrier = pltpu.get_barrier_semaphore()
    for there, device in i_side + j_side:

        @pl.when(there)
        def _():
            pl.semaphore_signal(barrier, inc=1, device_id=device, device_id_type=MESH)

    for device in stages[0] + stages[1]:
        pl.semaphore_signal(barrier, inc=1, device_id=device, device_id_type=MESH)

    load_flow = pltpu.make_async_copy(flow_ref, flow, load_sem.at[0])
    load_start = [
        pltpu.make_async_copy(
            start_ref.at[:, :, :, pl.ds(128 * c, 128)], v0.at[:, pl.ds(1, ni), c, rows, :], load_sem.at[1 + c]
        )
        for c in range(chunks)
    ]
    load_source = pltpu.make_async_copy(source_ref, source, load_sem.at[1 + chunks])
    load_precond = [
        pltpu.make_async_copy(precond_ref.at[u], precond.at[u], load_sem.at[2 + chunks + u]) for u in range(NV)
    ]
    load_jac = pltpu.make_async_copy(jac_ref, jac, load_sem.at[2 + chunks + NV])
    load_codes = pltpu.make_async_copy(codes_ref, codes, load_sem.at[3 + chunks + NV])
    for copy in [load_codes, load_jac, load_flow, *load_start, load_source, *load_precond]:
        copy.start()

    def halo_i(buffer, sweep, side, first, count, source_of=None):
        own, other = (1, ni + 1) if side == 0 else (ni, 0)
        if source_of is None:
            lead = slice(None), own, pl.ds(first, count), rows, slice(None)
            src = buffer.at[lead]
            dst = buffer.at[:, other, pl.ds(first, count), rows, :]
        else:
            src = source_of.at[:, own - 1, :, pl.ds(128 * first, 128)]
            dst = buffer.at[:, other, first, rows, :]
        return pltpu.make_async_remote_copy(
            src_ref=src, dst_ref=dst, send_sem=i_send.at[sweep, side, first],
            recv_sem=i_recv.at[sweep, 1 - side, first], device_id=i_side[side][1], device_id_type=MESH,
        )

    def halo_j(buffer, piece, side, first, count):
        own, other = (J0, J0 + nj) if side == 0 else (J0 + nj - 1, J0 - 1)
        planes = pl.ds(1 + first, count)
        return pltpu.make_async_remote_copy(
            src_ref=buffer.at[:, planes, :, pl.ds(own, 1), :], dst_ref=buffer.at[:, planes, :, pl.ds(other, 1), :],
            send_sem=j_send.at[piece, side], recv_sem=j_recv.at[piece, 1 - side],
            device_id=j_side[side][1], device_id_type=MESH,
        )

    def halo_speed(axis, side):
        if axis == 0:
            own, other = (1, ni + 1) if side == 0 else (ni, 0)
            src, dst = speed.at[own, :, rows, :], speed.at[other, :, rows, :]
            device = i_side[side][1]
        else:
            own, other = (J0, J0 + nj) if side == 0 else (J0 + nj - 1, J0 - 1)
            planes = pl.ds(1, ni)
            src, dst = speed.at[planes, :, pl.ds(own, 1), :], speed.at[planes, :, pl.ds(other, 1), :]
            device = j_side[side][1]
        return pltpu.make_async_remote_copy(
            src_ref=src, dst_ref=dst, send_sem=s_send.at[axis, side], recv_sem=s_recv.at[axis, 1 - side],
            device_id=device, device_id_type=MESH,
        )

    def on_sides(sides, make, act):
        for side in (0, 1):

            @pl.when(sides[side][0])
            def _():
                act(make, side)

    def start(make, side):
        make(side).start()

    def arrived(make, side):
        make(1 - side).wait_recv()

    def sent(make, side):
        make(side).wait_send()

    zero_plane = jnp.zeros((chunks, nj, 128), jnp.float32)
    zero_rows = jnp.zeros((1, 128), jnp.float32)
    for side in (0, 1):
        plane, row = (0, J0 - 1) if side == 0 else (ni + 1, J0 + nj)

        @pl.when(jnp.logical_not(i_side[side][0]))
        def _():
            speed[plane, :, rows, :] = zero_plane
            for u in range(NV):
                v0[u, plane, :, rows, :] = zero_plane
                v1[u, plane, :, rows, :] = zero_plane

        @pl.when(jnp.logical_not(j_side[side][0]))
        def _():
            def clear(i, carry):
                for c in range(chunks):
                    speed[i + 1, c, pl.ds(row, 1), :] = zero_rows
                    for u in range(NV):
                        v0[u, i + 1, c, pl.ds(row, 1), :] = zero_rows
                        v1[u, i + 1, c, pl.ds(row, 1), :] = zero_rows
                return carry

            lax.fori_loop(0, ni, clear, 0)

    lane = lax.broadcasted_iota(jnp.int32, (nj, 128), 1)
    diagonal = lax.broadcasted_iota(jnp.int32, (nj, nj), 0) == lax.broadcasted_iota(jnp.int32, (nj, nj), 1)
    load_codes.wait()
    for i in range(ni):
        line = jnp.broadcast_to(codes[i : i + 1, :].astype(jnp.float32), (nj, nj))
        column = jnp.sum(jnp.where(diagonal, line, 0.0), axis=1, keepdims=True)
        column = jnp.broadcast_to(column, (nj, 128))
        ghost[i] = jnp.where(column == 1.0, 0.0, -1.0)
        flip[i] = jnp.where((column == 0.0) & (lane == 0), 2.0, 0.0)

    peers = sum(len(stage) for stage in stages)
    for there, _ in i_side + j_side:
        peers = peers + jnp.where(there, 1, 0)
    pl.semaphore_wait(barrier, peers)

    for c in range(chunks):
        on_sides(i_side, lambda side: halo_i(v0, 0, side, c, 1, start_ref), start)

    load_flow.wait()

    def speeds(i):
        density = flow[0, i]
        momentum = flow[1, i] * flow[1, i] + flow[2, i] * flow[2, i] + flow[3, i] * flow[3, i]
        quarter = 0.25 * (jnp.sqrt(momentum) / density + jnp.sqrt(1.4 * flow[4, i] / density))
        for c in range(chunks):
            speed[i + 1, c, rows, :] = quarter[:, 128 * c : 128 * c + 128]

    def loop_speeds(first, count, stride):
        def step(t, carry):
            speeds(first + stride * t)
            return carry

        lax.fori_loop(0, count, step, 0)

    loop_speeds(0, 2, ni - 1)
    on_sides(i_side, functools.partial(halo_speed, 0), start)
    for copy in load_start:
        copy.wait()
    on_sides(j_side, lambda side: halo_j(v0, 0, side, 0, ni), start)
    loop_speeds(1, ni - 2, 1)
    on_sides(j_side, functools.partial(halo_speed, 1), start)

    load_jac.wait()
    half = [[[0.5 * jac[u, d, v] for v in range(NV)] for u in range(NV)] for d in range(3)]

    def along_k(read, h, mirror):
        own = [read(2 * h), read(2 * h + 1)]
        up = [pltpu.roll(x, 1, 1) for x in own]
        down = [pltpu.roll(x, 127, 1) for x in own]
        before = mirror * own[0] if h == 0 else pltpu.roll(read(2 * h - 1), 1, 1)
        after = jnp.zeros_like(own[0]) if 2 * h + 2 == chunks else pltpu.roll(read(2 * h + 2), 127, 1)
        first, last = lane == 0, lane == 127
        left = [jnp.where(first, before, up[0]), jnp.where(first, up[0], up[1])]
        right = [jnp.where(last, down[1], down[0]), jnp.where(last, after, down[1])]
        return own, left, right

    def update(v, i, h, store):
        mirror = ghost[i]
        s_own, s_left, s_right = along_k(lambda c: speed[i + 1, c, rows, :], h, mirror)
        around = [along_k(lambda c, u=u: v[u, i + 1, c, rows, :], h, mirror) for u in range(NV)]
        squares = jnp.zeros((nj, 128), jnp.float32)
        for q in (0, 1):
            c = 2 * h + q
            own = [around[u][0][q] for u in range(NV)]
            s = s_own[q]
            places = [
                (speed[i, c, rows, :], lambda u, c=c: v[u, i, c, rows, :]),
                (speed[i + 2, c, rows, :], lambda u, c=c: v[u, i + 2, c, rows, :]),
                (speed[i + 1, c, pl.ds(J0 - 1, nj), :], lambda u, c=c: v[u, i + 1, c, pl.ds(J0 - 1, nj), :]),
                (speed[i + 1, c, pl.ds(J0 + 1, nj), :], lambda u, c=c: v[u, i + 1, c, pl.ds(J0 + 1, nj), :]),
                (s_left[q], lambda u, q=q: around[u][1][q]),
                (s_right[q], lambda u, q=q: around[u][2][q]),
            ]
            weights = [s + beside for beside, _ in places]
            total = functools.reduce(jnp.add, weights)
            r = [source[u, i, :, 128 * c : 128 * c + 128] - total * own[u] for u in range(NV)]
            for d in range(3):
                jump = []
                for u in range(NV):
                    low, high = places[2 * d][1](u), places[2 * d + 1][1](u)
                    r[u] = r[u] + (weights[2 * d] * low + weights[2 * d + 1] * high)
                    jump.append(high - low)
                for w in range(NV):
                    for u in range(NV):
                        r[w] = r[w] + half[d][u][w] * jump[u]
            if c == 0:
                wall = s * own[3]
                for u in range(NV):
                    wall = wall + half[2][u][3] * own[u]
                r[3] = r[3] - flip[i] * wall
            for w in range(NV):
                new = own[w]
                for u in range(NV):
                    new = new + precond[u, w, i, :, 128 * c : 128 * c + 128] * r[u]
                store(w, c, new)
                squares = squares + r[w] * r[w]
        return squares

    def planes(v, first, count, stride, halves, store, squares):
        def step(t, carry):
            i = first + stride * t
            for h in halves:
                carry = carry + update(v, i, h, functools.partial(store, i))
            return carry

        return lax.fori_loop(0, count, step, squares)

    def store_v1(i, w, c, new):
        v1[w, i + 1, c, rows, :] = new

    def store_out(i, w, c, new):
        out[w, i, :, 128 * c : 128 * c + 128] = new

    load_source.wait()
    for copy in load_precond:
        copy.wait()

    none = jnp.zeros((nj, 128), jnp.float32)
    halves = tuple(range(chunks // 2))

    on_sides(j_side, functools.partial(halo_speed, 1), arrived)
    on_sides(j_side, lambda side: halo_j(v0, 0, side, 0, ni), arrived)
    squares0 = planes(v0, 1, ni - 2, 1, halves, store_v1, none)
    inner_j = lambda side: halo_j(v1, 1, side, 1, ni - 2)
    on_sides(j_side, inner_j, start)
    on_sides(i_side, functools.partial(halo_speed, 0), arrived)
    for h in halves:
        for c in (2 * h, 2 * h + 1):
            on_sides(i_side, lambda side: halo_i(v0, 0, side, c, 1, start_ref), arrived)
        squares0 = planes(v0, 0, 2, ni - 1, (h,), store_v1, squares0)
        on_sides(i_side, lambda side: halo_i(v1, 1, side, 2 * h, 2), start)
    outer_j = [lambda side: halo_j(v1, 2, side, 0, 1), lambda side: halo_j(v1, 3, side, ni - 1, 1)]
    for make in outer_j:
        on_sides(j_side, make, start)

    on_sides(j_side, inner_j, arrived)
    squares1 = planes(v1, 1, ni - 2, 1, halves, store_out, none)
    for make in outer_j:
        on_sides(j_side, make, arrived)
    for h in halves:
        on_sides(i_side, lambda side: halo_i(v1, 1, side, 2 * h, 2), arrived)
        squares1 = planes(v1, 0, 2, ni - 1, (h,), store_out, squares1)

    row = lax.broadcasted_iota(jnp.int32, (8, 128), 0)
    sums = jnp.where(
        row == 0,
        jnp.sum(squares0, axis=0, keepdims=True),
        jnp.where(row == 1, jnp.sum(squares1, axis=0, keepdims=True), 0.0),
    )
    reduction = []
    slot = 0
    for number, stage in enumerate(stages):
        part[number] = sums
        copies = []
        for device in stage:
            copy = pltpu.make_async_remote_copy(
                src_ref=part.at[number], dst_ref=gathered.at[slot], send_sem=r_send.at[slot],
                recv_sem=r_recv.at[slot], device_id=device, device_id_type=MESH,
            )
            copy.start()
            copies.append((slot, copy))
            slot += 1
        for where, copy in copies:
            copy.wait_recv()
            sums = sums + gathered[where]
        reduction += [copy for _, copy in copies]
    root = jnp.sqrt(jnp.sum(sums, axis=1, keepdims=True) / cells_all)
    rms_ref[0] = root[0, 0]
    rms_ref[1] = root[1, 0]

    for copy in reduction:
        copy.wait_send()
    for c in range(chunks):
        on_sides(i_side, lambda side: halo_i(v0, 0, side, c, 1, start_ref), sent)
    for h in halves:
        on_sides(i_side, lambda side: halo_i(v1, 1, side, 2 * h, 2), sent)
    on_sides(j_side, lambda side: halo_j(v0, 0, side, 0, ni), sent)
    for make in [inner_j, *outer_j]:
        on_sides(j_side, make, sent)
    on_sides(i_side, functools.partial(halo_speed, 0), sent)
    on_sides(j_side, functools.partial(halo_speed, 1), sent)


def per_device(adjoint_start, source, flow_state, precond, flux_jac, bc_codes):
    nv, ni, nj, nk = adjoint_start.shape
    cells_all = float(adjoint_start.size * lax.axis_size("stream") * lax.axis_size("span"))
    padded = (ni + 2, nk // 128, nj + 2 * J0, 128)
    hbm = pl.BlockSpec(memory_space=pltpu.HBM)
    in_hbm = functools.partial(pltpu.with_memory_space_constraint, memory_space=pltpu.HBM)
    dma = pltpu.SemaphoreType.DMA
    return pl.pallas_call(
        functools.partial(kernel, cells_all),
        out_shape=(
            pltpu.VMEM(adjoint_start.shape, jnp.float32),
            jax.ShapeDtypeStruct((2,), jnp.float32),
        ),
        in_specs=[hbm, hbm, hbm, hbm, hbm, hbm],
        out_specs=(pl.BlockSpec(memory_space=pltpu.VMEM), pl.BlockSpec(memory_space=pltpu.SMEM)),
        scratch_shapes=[
            pltpu.VMEM((nv, *padded), jnp.float32),
            pltpu.VMEM((nv, *padded), jnp.float32),
            pltpu.VMEM(padded, jnp.float32),
            pltpu.VMEM(flow_state.shape, jnp.float32),
            pltpu.VMEM(source.shape, jnp.float32),
            pltpu.VMEM(precond.shape, jnp.float32),
            pltpu.SMEM((nv, 3, nv), jnp.float32),
            pltpu.VMEM(bc_codes.shape, jnp.int32),
            pltpu.VMEM((ni, nj, 128), jnp.float32),
            pltpu.VMEM((ni, nj, 128), jnp.float32),
            pltpu.VMEM((2, 8, 128), jnp.float32),
            pltpu.VMEM((30, 8, 128), jnp.float32),
            dma((16,)),
            dma((2, 2, nk // 128)),
            dma((2, 2, nk // 128)),
            dma((4, 2)),
            dma((4, 2)),
            dma((2, 2)),
            dma((2, 2)),
            dma((30,)),
            dma((30,)),
        ],
        compiler_params=pltpu.CompilerParams(
            collective_id=0, has_side_effects=True, vmem_limit_bytes=40 * 1024 * 1024
        ),
        cost_estimate=pl.CostEstimate(flops=40_000_000, bytes_accessed=13_000_000, transcendentals=131072),
        name="jacobi_sweeps",
    )(*map(in_hbm, (adjoint_start, source, flow_state, precond, jnp.transpose(flux_jac, (1, 0, 2)), bc_codes)))


def solution(mesh):
    split = P(None, "stream", "span", None)
    return jax.shard_map(
        per_device,
        mesh=mesh,
        in_specs=(split, split, split, P(None, None, "stream", "span", None), P(), P("stream", "span")),
        out_specs=(split, P()),
        check_vma=False,
    )
```

profile of v0, /device:TPU:1, one launch (start us, length us, event | category | flops | bytes accessed | tf_op | source)
XLA Modules:
  0.0 42.1 jit_solution(4052434187021473029)
XLA Ops:
  0.6 39.9 %jacobi_sweeps.1 = (f32[5,8,16,512]{3,2,1,0:T(8,128)S(1)}, f32[2]{0:T(128)S(1)}) custom-call(f32[5,8,16,512]{3,2,1,0:T(8,128)} %start_ref.1, f32[5,8,16,512]{3,2,1,0:T(8,128)} %source_ref.1, f32[5,8,16,512]{3,2,1,0:T(8,128)} %flow_ref.1, f32[5,5,8,16,512]{4,3,2,1,0:T(8,128)} %precond_ref.1, f32[5,3,5]{2,1,0:T(4,128)} %bitcast.1, s32[8,16]{1,0:T(8,128)} %codes_ref.1), custom_call_target="tpu_custom_call" | custom-call | flops 40000000 | bytes 13000000 | tf_op jit(solution)/shard_map/jacobi_sweeps/pallas_call | solution.py:343
  40.6 1.1 %copy.10 = f32[5,8,16,512]{3,2,1,0:T(8,128)} copy(f32[5,8,16,512]{3,2,1,0:T(8,128)S(1)} %get-tuple-element.2) | data formatting | bytes 2621440
  41.6 0.5 %copy.11 = f32[2]{0:T(128)} copy(f32[2]{0:T(128)S(1)} %get-tuple-element.7) | data formatting | bytes 16
where the time goes:
time: 42.2 us; the launch traced here: 42.1 us
  Pallas kernels  39.9 us (95%)
  local copies, waits for them, and re-layouts  1.57 us (4%)
  between operations  0.64 us (2%)
    pallas_call x1, Pallas kernels, per_device(): pl.pallas_call(functools.partial(kernel, cells_all), out_shape=(pltpu.VME...  39.9 us
    unnamed x2, local copies, waits for them, and re-layouts  1.57 us

commit v1 on v0

--- a/solution.py
+++ b/solution.py
@@ -32,7 +32,7 @@
 
 
 def kernel(
-    cells_all, start_ref, source_ref, flow_ref, precond_ref, jac_ref, codes_ref, out, rms_ref,
+    start_ref, source_ref, flow_ref, precond_ref, jac_ref, codes_ref, out, sums_ref,
     v0, v1, speed, flow, source, precond, jac, codes, ghost, flip, part, gathered,
     load_sem, i_send, i_recv, j_send, j_recv, s_send, s_recv, r_send, r_recv,
 ):
@@ -160,14 +160,6 @@
         ghost[i] = jnp.where(column == 1.0, 0.0, -1.0)
         flip[i] = jnp.where((column == 0.0) & (lane == 0), 2.0, 0.0)
 
-    peers = sum(len(stage) for stage in stages)
-    for there, _ in i_side + j_side:
-        peers = peers + jnp.where(there, 1, 0)
-    pl.semaphore_wait(barrier, peers)
-
-    for c in range(chunks):
-        on_sides(i_side, lambda side: halo_i(v0, 0, side, c, 1, start_ref), start)
-
     load_flow.wait()
 
     def speeds(i):
@@ -184,13 +176,20 @@
 
         lax.fori_loop(0, count, step, 0)
 
-    loop_speeds(0, 2, ni - 1)
-    on_sides(i_side, functools.partial(halo_speed, 0), start)
+    loop_speeds(0, ni, 1)
     for copy in load_start:
         copy.wait()
+
+    peers = sum(len(stage) for stage in stages)
+    for there, _ in i_side + j_side:
+        peers = peers + jnp.where(there, 1, 0)
+    pl.semaphore_wait(barrier, peers)
+
     on_sides(j_side, lambda side: halo_j(v0, 0, side, 0, ni), start)
-    loop_speeds(1, ni - 2, 1)
     on_sides(j_side, functools.partial(halo_speed, 1), start)
+    on_sides(i_side, functools.partial(halo_speed, 0), start)
+    for c in range(chunks):
+        on_sides(i_side, lambda side: halo_i(v0, 0, side, c, 1, start_ref), start)
 
     load_jac.wait()
     half = [[[0.5 * jac[u, d, v] for v in range(NV)] for u in range(NV)] for d in range(3)]
@@ -316,9 +315,7 @@
             copy.wait_recv()
             sums = sums + gathered[where]
         reduction += [copy for _, copy in copies]
-    root = jnp.sqrt(jnp.sum(sums, axis=1, keepdims=True) / cells_all)
-    rms_ref[0] = root[0, 0]
-    rms_ref[1] = root[1, 0]
+    sums_ref[...] = sums
 
     for copy in reduction:
         copy.wait_send()
@@ -333,21 +330,30 @@
     on_sides(j_side, functools.partial(halo_speed, 1), sent)
 
 
+def deliver(cells_all, adjoint_vmem, sums_ref, adjoint_ref, rms_ref, sem):
+    copy = pltpu.make_async_copy(adjoint_vmem, adjoint_ref, sem)
+    copy.start()
+    root = jnp.sqrt(jnp.sum(sums_ref[...], axis=1, keepdims=True) / cells_all)
+    rms_ref[0] = root[0, 0]
+    rms_ref[1] = root[1, 0]
+    copy.wait()
+
+
 def per_device(adjoint_start, source, flow_state, precond, flux_jac, bc_codes):
     nv, ni, nj, nk = adjoint_start.shape
     cells_all = float(adjoint_start.size * lax.axis_size("stream") * lax.axis_size("span"))
     padded = (ni + 2, nk // 128, nj + 2 * J0, 128)
-    hbm = pl.BlockSpec(memory_space=pltpu.HBM)
+    hbm, vmem = pl.BlockSpec(memory_space=pltpu.HBM), pl.BlockSpec(memory_space=pltpu.VMEM)
     in_hbm = functools.partial(pltpu.with_memory_space_constraint, memory_space=pltpu.HBM)
     dma = pltpu.SemaphoreType.DMA
-    return pl.pallas_call(
-        functools.partial(kernel, cells_all),
+    adjoint, sums = pl.pallas_call(
+        kernel,
         out_shape=(
             pltpu.VMEM(adjoint_start.shape, jnp.float32),
-            jax.ShapeDtypeStruct((2,), jnp.float32),
+            pltpu.VMEM((8, 128), jnp.float32),
         ),
         in_specs=[hbm, hbm, hbm, hbm, hbm, hbm],
-        out_specs=(pl.BlockSpec(memory_space=pltpu.VMEM), pl.BlockSpec(memory_space=pltpu.SMEM)),
+        out_specs=(vmem, vmem),
         scratch_shapes=[
             pltpu.VMEM((nv, *padded), jnp.float32),
             pltpu.VMEM((nv, *padded), jnp.float32),
@@ -377,6 +383,18 @@
         cost_estimate=pl.CostEstimate(flops=40_000_000, bytes_accessed=13_000_000, transcendentals=131072),
         name="jacobi_sweeps",
     )(*map(in_hbm, (adjoint_start, source, flow_state, precond, jnp.transpose(flux_jac, (1, 0, 2)), bc_codes)))
+    return pl.pallas_call(
+        functools.partial(deliver, cells_all),
+        out_shape=(
+            jax.ShapeDtypeStruct(adjoint.shape, jnp.float32),
+            jax.ShapeDtypeStruct((2,), jnp.float32),
+        ),
+        in_specs=[vmem, vmem],
+        out_specs=(hbm, pl.BlockSpec(memory_space=pltpu.SMEM)),
+        scratch_shapes=[dma],
+        compiler_params=pltpu.CompilerParams(vmem_limit_bytes=4 * 1024 * 1024),
+        name="deliver",
+    )(*(pltpu.with_memory_space_constraint(x, memory_space=pltpu.VMEM) for x in (adjoint, sums)))
 
 
 def solution(mesh):

time: 42.2 us -> 39.1 us (0.927)
  Pallas kernels: 39.9 us -> 38.3 us
  local copies, waits for them, and re-layouts: 1.57 us -> 0 us
    pallas_call x1 -> x2, Pallas kernels: 39.9 us -> 38.3 us  [the longest x1 36.8 us: per_device(): pl.pallas_call(kernel, out_shape=(pltpu.VMEM(adjoint_start.shape, jnp.flo...]
    unnamed x2 -> x0, local copies, waits for them, and re-layouts: 1.57 us -> none
where the time goes in v1:
time: 39.1 us; the launch traced here: 39 us
  Pallas kernels  38.3 us (98%)
  between operations  0.64 us (2%)
    pallas_call x1, Pallas kernels, per_device(): pl.pallas_call(kernel, out_shape=(pltpu.VMEM(adjoint_start.shape, jnp.flo...  36.8 us
    pallas_call x1, Pallas kernels, per_device(): pl.pallas_call(functools.partial(deliver, cells_all), out_shape=(jax.Shap...  1.58 us

profile of v1, /device:TPU:1, one launch (start us, length us, event | category | flops | bytes accessed | tf_op | source)
XLA Modules:
  0.0 39.0 jit_solution(11957389733370510256)
XLA Ops:
  0.6 36.8 %jacobi_sweeps.1 = (f32[5,8,16,512]{3,2,1,0:T(8,128)S(1)}, f32[8,128]{1,0:T(8,128)S(1)}) custom-call(f32[5,8,16,512]{3,2,1,0:T(8,128)} %start_ref.1, f32[5,8,16,512]{3,2,1,0:T(8,128)} %source_ref.1, f32[5,8,16,512]{3,2,1,0:T(8,128)} %flow_ref.1, f32[5,5,8,16,512]{4,3,2,1,0:T(8,128)} %precond_ref.1, f32[5,3,5]{2,1,0:T(4,128)} %bitcast.1, s32[8,16]{1,0:T(8,128)} %codes_ref.1), custom_call_target="tpu_custom_call" | custom-call | flops 40000000 | bytes 13000000 | tf_op jit(solution)/shard_map/jacobi_sweeps/pallas_call | solution.py:349
  37.4 1.6 %deliver.1 = (f32[5,8,16,512]{3,2,1,0:T(8,128)}, f32[2]{0:T(128)}) custom-call(f32[5,8,16,512]{3,2,1,0:T(8,128)S(1)} %get-tuple-element.4.adjoint_vmem, f32[8,128]{1,0:T(8,128)S(1)} %get-tuple-element.5.sums_ref), custom_call_target="tpu_custom_call" | custom-call | tf_op jit(solution)/shard_map/deliver/pallas_call | solution.py:386

commit v2 on v1

--- a/solution.py
+++ b/solution.py
@@ -33,7 +33,7 @@
 
 def kernel(
     start_ref, source_ref, flow_ref, precond_ref, jac_ref, codes_ref, out, sums_ref,
-    v0, v1, speed, flow, source, precond, jac, codes, ghost, flip, part, gathered,
+    v0, v1, speed, i_in, j_in, s_i_in, s_j_in, residual, flow, source, precond, jac, codes, ghost, flip, part, gathered,
     load_sem, i_send, i_recv, j_send, j_recv, s_send, s_recv, r_send, r_recv,
 ):
     stream, span = lax.axis_index("stream"), lax.axis_index("span")
@@ -72,43 +72,36 @@
     for copy in [load_codes, load_jac, load_flow, *load_start, load_source, *load_precond]:
         copy.start()
 
-    def halo_i(buffer, sweep, side, first, count, source_of=None):
-        own, other = (1, ni + 1) if side == 0 else (ni, 0)
-        if source_of is None:
-            lead = slice(None), own, pl.ds(first, count), rows, slice(None)
-            src = buffer.at[lead]
-            dst = buffer.at[:, other, pl.ds(first, count), rows, :]
+    def remote(src, dst, send_sem, recv_sem, device):
+        return pltpu.make_async_remote_copy(
+            src_ref=src, dst_ref=dst, send_sem=send_sem, recv_sem=recv_sem, device_id=device, device_id_type=MESH
+        )
+
+    def halo_i(sweep, side, first, count):
+        own = 0 if side == 0 else ni - 1
+        if sweep == 0:
+            src = start_ref.at[:, own, :, pl.ds(128 * first, 128)]
+            dst = i_in.at[0, 1 - side, :, first]
         else:
-            src = source_of.at[:, own - 1, :, pl.ds(128 * first, 128)]
-            dst = buffer.at[:, other, first, rows, :]
-        return pltpu.make_async_remote_copy(
-            src_ref=src, dst_ref=dst, send_sem=i_send.at[sweep, side, first],
-            recv_sem=i_recv.at[sweep, 1 - side, first], device_id=i_side[side][1], device_id_type=MESH,
-        )
-
-    def halo_j(buffer, piece, side, first, count):
-        own, other = (J0, J0 + nj) if side == 0 else (J0 + nj - 1, J0 - 1)
-        planes = pl.ds(1 + first, count)
-        return pltpu.make_async_remote_copy(
-            src_ref=buffer.at[:, planes, :, pl.ds(own, 1), :], dst_ref=buffer.at[:, planes, :, pl.ds(other, 1), :],
-            send_sem=j_send.at[piece, side], recv_sem=j_recv.at[piece, 1 - side],
-            device_id=j_side[side][1], device_id_type=MESH,
-        )
+            src = v1.at[:, own + 1, pl.ds(first, count), rows, :]
+            dst = i_in.at[1, 1 - side, :, pl.ds(first, count)]
+        return remote(src, dst, i_send.at[sweep, side, first], i_recv.at[sweep, 1 - side, first], i_side[side][1])
+
+    def halo_j(sweep, piece, side, first, count):
+        own, other = (0, nj - 1) if side == 0 else (nj - 1, 0)
+        src = (v0, v1)[sweep].at[:, pl.ds(1 + first, count), :, pl.ds(J0 + own, 1), :]
+        dst = j_in.at[sweep, :, pl.ds(first, count), :, pl.ds(other, 1), :]
+        return remote(src, dst, j_send.at[piece, side], j_recv.at[piece, 1 - side], j_side[side][1])
 
     def halo_speed(axis, side):
         if axis == 0:
-            own, other = (1, ni + 1) if side == 0 else (ni, 0)
-            src, dst = speed.at[own, :, rows, :], speed.at[other, :, rows, :]
+            src, dst = speed.at[1 if side == 0 else ni, :, rows, :], s_i_in.at[1 - side]
             device = i_side[side][1]
         else:
-            own, other = (J0, J0 + nj) if side == 0 else (J0 + nj - 1, J0 - 1)
-            planes = pl.ds(1, ni)
-            src, dst = speed.at[planes, :, pl.ds(own, 1), :], speed.at[planes, :, pl.ds(other, 1), :]
+            own, other = (0, nj - 1) if side == 0 else (nj - 1, 0)
+            src, dst = speed.at[pl.ds(1, ni), :, pl.ds(J0 + own, 1), :], s_j_in.at[:, :, pl.ds(other, 1), :]
             device = j_side[side][1]
-        return pltpu.make_async_remote_copy(
-            src_ref=src, dst_ref=dst, send_sem=s_send.at[axis, side], recv_sem=s_recv.at[axis, 1 - side],
-            device_id=device, device_id_type=MESH,
-        )
+        return remote(src, dst, s_send.at[axis, side], s_recv.at[axis, 1 - side], device)
 
     def on_sides(sides, make, act):
         for side in (0, 1):
@@ -127,25 +120,42 @@
         make(side).wait_send()
 
     zero_plane = jnp.zeros((chunks, nj, 128), jnp.float32)
-    zero_rows = jnp.zeros((1, 128), jnp.float32)
+    zero_row = jnp.zeros((1, 128), jnp.float32)
+    for plane in (0, ni + 1):
+        speed[plane, :, rows, :] = zero_plane
+        for u in range(NV):
+            v0[u, plane, :, rows, :] = zero_plane
+            v1[u, plane, :, rows, :] = zero_plane
+
+    def clear_beside(i, carry):
+        for c in range(chunks):
+            for row in (J0 - 1, J0 + nj):
+                speed[i + 1, c, pl.ds(row, 1), :] = zero_row
+                for u in range(NV):
+                    v0[u, i + 1, c, pl.ds(row, 1), :] = zero_row
+                    v1[u, i + 1, c, pl.ds(row, 1), :] = zero_row
+        return carry
+
+    lax.fori_loop(0, ni, clear_beside, 0)
     for side in (0, 1):
-        plane, row = (0, J0 - 1) if side == 0 else (ni + 1, J0 + nj)
 
         @pl.when(jnp.logical_not(i_side[side][0]))
         def _():
-            speed[plane, :, rows, :] = zero_plane
+            s_i_in[side] = zero_plane
             for u in range(NV):
-                v0[u, plane, :, rows, :] = zero_plane
-                v1[u, plane, :, rows, :] = zero_plane
+                i_in[0, side, u] = zero_plane
+                i_in[1, side, u] = zero_plane
 
         @pl.when(jnp.logical_not(j_side[side][0]))
         def _():
+            row = 0 if side == 0 else nj - 1
+
             def clear(i, carry):
                 for c in range(chunks):
-                    speed[i + 1, c, pl.ds(row, 1), :] = zero_rows
+                    s_j_in[i, c, pl.ds(row, 1), :] = zero_row
                     for u in range(NV):
-                        v0[u, i + 1, c, pl.ds(row, 1), :] = zero_rows
-                        v1[u, i + 1, c, pl.ds(row, 1), :] = zero_rows
+                        j_in[0, u, i, c, pl.ds(row, 1), :] = zero_row
+                        j_in[1, u, i, c, pl.ds(row, 1), :] = zero_row
                 return carry
 
             lax.fori_loop(0, ni, clear, 0)
@@ -185,11 +195,11 @@
         peers = peers + jnp.where(there, 1, 0)
     pl.semaphore_wait(barrier, peers)
 
-    on_sides(j_side, lambda side: halo_j(v0, 0, side, 0, ni), start)
+    on_sides(j_side, lambda side: halo_j(0, 0, side, 0, ni), start)
     on_sides(j_side, functools.partial(halo_speed, 1), start)
     on_sides(i_side, functools.partial(halo_speed, 0), start)
     for c in range(chunks):
-        on_sides(i_side, lambda side: halo_i(v0, 0, side, c, 1, start_ref), start)
+        on_sides(i_side, lambda side: halo_i(0, side, c, 1), start)
 
     load_jac.wait()
     half = [[[0.5 * jac[u, d, v] for v in range(NV)] for u in range(NV)] for d in range(3)]
@@ -205,11 +215,10 @@
         right = [jnp.where(last, down[1], down[0]), jnp.where(last, after, down[1])]
         return own, left, right
 
-    def update(v, i, h, store):
+    def inside(v, i, h):
         mirror = ghost[i]
         s_own, s_left, s_right = along_k(lambda c: speed[i + 1, c, rows, :], h, mirror)
         around = [along_k(lambda c, u=u: v[u, i + 1, c, rows, :], h, mirror) for u in range(NV)]
-        squares = jnp.zeros((nj, 128), jnp.float32)
         for q in (0, 1):
             c = 2 * h + q
             own = [around[u][0][q] for u in range(NV)]
@@ -239,64 +248,121 @@
                 for u in range(NV):
                     wall = wall + half[2][u][3] * own[u]
                 r[3] = r[3] - flip[i] * wall
-            for w in range(NV):
-                new = own[w]
-                for u in range(NV):
-                    new = new + precond[u, w, i, :, 128 * c : 128 * c + 128] * r[u]
-                store(w, c, new)
-                squares = squares + r[w] * r[w]
-        return squares
-
-    def planes(v, first, count, stride, halves, store, squares):
-        def step(t, carry):
-            i = first + stride * t
+            for u in range(NV):
+                residual[u, i, c] = r[u]
+
+    row = lax.broadcasted_iota(jnp.int32, (nj, 128), 0)
+    edge = (row == 0) | (row == nj - 1)
+    edge_sign = jnp.where(row < nj // 2, -1.0, 1.0)
+
+    def add_beside(r, s, own, s_beside, beside, d, sign):
+        weight = s + s_beside
+        signed = [sign * x for x in beside]
+        for w in range(NV):
+            r[w] = r[w] + (weight * beside[w] - s_beside * own[w])
+            for u in range(NV):
+                r[w] = r[w] + half[d][u][w] * signed[u]
+
+    def whole(v, sweep, i, c, side):
+        r = [residual[u, i, c] for u in range(NV)]
+        s = speed[i + 1, c, rows, :]
+        own = [v[u, i + 1, c, rows, :] for u in range(NV)]
+        beside = [jnp.where(edge, j_in[sweep, u, i, c], 0.0) for u in range(NV)]
+        add_beside(r, s, own, jnp.where(edge, s_j_in[i, c], 0.0), beside, 1, edge_sign)
+        if side is not None:
+            beside = [i_in[sweep, side, u, c] for u in range(NV)]
+            add_beside(r, s, own, s_i_in[side, c], beside, 0, (2 * side - 1).astype(jnp.float32))
+        return r, own
+
+    def preconditioned(r, own, i, c):
+        new = []
+        for w in range(NV):
+            total = own[w]
+            for u in range(NV):
+                total = total + precond[u, w, i, :, 128 * c : 128 * c + 128] * r[u]
+            new.append(total)
+        return new
+
+    def first_sweep(i, c, side, squares):
+        r, own = whole(v0, 0, i, c, side)
+        for w, new in enumerate(preconditioned(r, own, i, c)):
+            v1[w, i + 1, c, rows, :] = new
+        return squares + functools.reduce(jnp.add, [x * x for x in r])
+
+    def second_sweep(i, c, side, squares):
+        r, _ = whole(v1, 1, i, c, side)
+        for u in range(NV):
+            residual[u, i, c] = r[u]
+        return squares + functools.reduce(jnp.add, [x * x for x in r])
+
+    def all_inside(v):
+        def step(i, carry):
             for h in halves:
-                carry = carry + update(v, i, h, functools.partial(store, i))
+                inside(v, i, h)
             return carry
 
-        return lax.fori_loop(0, count, step, squares)
-
-    def store_v1(i, w, c, new):
-        v1[w, i + 1, c, rows, :] = new
-
-    def store_out(i, w, c, new):
-        out[w, i, :, 128 * c : 128 * c + 128] = new
+        lax.fori_loop(0, ni, step, 0)
+
+    def inner_planes(act, squares):
+        def step(i, carry):
+            for c in range(chunks):
+                carry = act(i, c, None, carry)
+            return carry
+
+        return lax.fori_loop(1, ni - 1, step, squares)
+
+    def outer_planes(act, h, squares):
+        def step(side, carry):
+            for c in (2 * h, 2 * h + 1):
+                carry = act((ni - 1) * side, c, side, carry)
+            return carry
+
+        return lax.fori_loop(0, 2, step, squares)
+
+    none = jnp.zeros((nj, 128), jnp.float32)
+    halves = tuple(range(chunks // 2))
 
     load_source.wait()
+    all_inside(v0)
     for copy in load_precond:
         copy.wait()
-
-    none = jnp.zeros((nj, 128), jnp.float32)
-    halves = tuple(range(chunks // 2))
-
     on_sides(j_side, functools.partial(halo_speed, 1), arrived)
-    on_sides(j_side, lambda side: halo_j(v0, 0, side, 0, ni), arrived)
-    squares0 = planes(v0, 1, ni - 2, 1, halves, store_v1, none)
-    inner_j = lambda side: halo_j(v1, 1, side, 1, ni - 2)
+    on_sides(j_side, lambda side: halo_j(0, 0, side, 0, ni), arrived)
+    squares0 = inner_planes(first_sweep, none)
+    inner_j = lambda side: halo_j(1, 1, side, 1, ni - 2)
     on_sides(j_side, inner_j, start)
     on_sides(i_side, functools.partial(halo_speed, 0), arrived)
     for h in halves:
         for c in (2 * h, 2 * h + 1):
-            on_sides(i_side, lambda side: halo_i(v0, 0, side, c, 1, start_ref), arrived)
-        squares0 = planes(v0, 0, 2, ni - 1, (h,), store_v1, squares0)
-        on_sides(i_side, lambda side: halo_i(v1, 1, side, 2 * h, 2), start)
-    outer_j = [lambda side: halo_j(v1, 2, side, 0, 1), lambda side: halo_j(v1, 3, side, ni - 1, 1)]
+            on_sides(i_side, lambda side: halo_i(0, side, c, 1), arrived)
+        squares0 = outer_planes(first_sweep, h, squares0)
+        on_sides(i_side, lambda side: halo_i(1, side, 2 * h, 2), start)
+    outer_j = [lambda side: halo_j(1, 2, side, 0, 1), lambda side: halo_j(1, 3, side, ni - 1, 1)]
     for make in outer_j:
         on_sides(j_side, make, start)
 
+    all_inside(v1)
     on_sides(j_side, inner_j, arrived)
-    squares1 = planes(v1, 1, ni - 2, 1, halves, store_out, none)
+    squares1 = inner_planes(second_sweep, none)
     for make in outer_j:
         on_sides(j_side, make, arrived)
     for h in halves:
-        on_sides(i_side, lambda side: halo_i(v1, 1, side, 2 * h, 2), arrived)
-        squares1 = planes(v1, 0, 2, ni - 1, (h,), store_out, squares1)
-
-    row = lax.broadcasted_iota(jnp.int32, (8, 128), 0)
+        on_sides(i_side, lambda side: halo_i(1, side, 2 * h, 2), arrived)
+        squares1 = outer_planes(second_sweep, h, squares1)
+
+    def last(i, carry):
+        for c in range(chunks):
+            r = [residual[u, i, c] for u in range(NV)]
+            own = [v1[u, i + 1, c, rows, :] for u in range(NV)]
+            for w, new in enumerate(preconditioned(r, own, i, c)):
+                out[w, i, :, 128 * c : 128 * c + 128] = new
+        return carry
+
+    line = lax.broadcasted_iota(jnp.int32, (8, 128), 0)
     sums = jnp.where(
-        row == 0,
+        line == 0,
         jnp.sum(squares0, axis=0, keepdims=True),
-        jnp.where(row == 1, jnp.sum(squares1, axis=0, keepdims=True), 0.0),
+        jnp.where(line == 1, jnp.sum(squares1, axis=0, keepdims=True), 0.0),
     )
     reduction = []
     slot = 0
@@ -311,6 +377,8 @@
             copy.start()
             copies.append((slot, copy))
             slot += 1
+        if number == 0:
+            lax.fori_loop(0, ni, last, 0)
         for where, copy in copies:
             copy.wait_recv()
             sums = sums + gathered[where]
@@ -320,10 +388,10 @@
     for copy in reduction:
         copy.wait_send()
     for c in range(chunks):
-        on_sides(i_side, lambda side: halo_i(v0, 0, side, c, 1, start_ref), sent)
+        on_sides(i_side, lambda side: halo_i(0, side, c, 1), sent)
     for h in halves:
-        on_sides(i_side, lambda side: halo_i(v1, 1, side, 2 * h, 2), sent)
-    on_sides(j_side, lambda side: halo_j(v0, 0, side, 0, ni), sent)
+        on_sides(i_side, lambda side: halo_i(1, side, 2 * h, 2), sent)
+    on_sides(j_side, lambda side: halo_j(0, 0, side, 0, ni), sent)
     for make in [inner_j, *outer_j]:
         on_sides(j_side, make, sent)
     on_sides(i_side, functools.partial(halo_speed, 0), sent)
@@ -342,6 +410,7 @@
 def per_device(adjoint_start, source, flow_state, precond, flux_jac, bc_codes):
     nv, ni, nj, nk = adjoint_start.shape
     cells_all = float(adjoint_start.size * lax.axis_size("stream") * lax.axis_size("span"))
+    block = (ni, nk // 128, nj, 128)
     padded = (ni + 2, nk // 128, nj + 2 * J0, 128)
     hbm, vmem = pl.BlockSpec(memory_space=pltpu.HBM), pl.BlockSpec(memory_space=pltpu.VMEM)
     in_hbm = functools.partial(pltpu.with_memory_space_constraint, memory_space=pltpu.HBM)
@@ -358,6 +427,11 @@
             pltpu.VMEM((nv, *padded), jnp.float32),
             pltpu.VMEM((nv, *padded), jnp.float32),
             pltpu.VMEM(padded, jnp.float32),
+            pltpu.VMEM((2, 2, nv, nk // 128, nj, 128), jnp.float32),
+            pltpu.VMEM((2, nv, *block), jnp.float32),
+            pltpu.VMEM((2, nk // 128, nj, 128), jnp.float32),
+            pltpu.VMEM(block, jnp.float32),
+            pltpu.VMEM((nv, *block), jnp.float32),
             pltpu.VMEM(flow_state.shape, jnp.float32),
             pltpu.VMEM(source.shape, jnp.float32),
             pltpu.VMEM(precond.shape, jnp.float32),

time: 39.1 us -> 37.3 us (0.954)
  Pallas kernels: 38.3 us -> 36.6 us
    pallas_call x1, Pallas kernels: 36.8 us -> 35 us  [per_device(): pl.pallas_call(kernel, out_shape=(pltpu.VMEM(adjoint_start.shape, jnp.flo...]
where the time goes in v2:
time: 37.3 us; the launch traced here: 37.2 us
  Pallas kernels  36.6 us (98%)
  between operations  0.64 us (2%)
    pallas_call x1, Pallas kernels, per_device(): pl.pallas_call(kernel, out_shape=(pltpu.VMEM(adjoint_start.shape, jnp.flo...  35 us
    pallas_call x1, Pallas kernels, per_device(): pl.pallas_call(functools.partial(deliver, cells_all), out_shape=(jax.Shap...  1.58 us

profile of v2, /device:TPU:1, one launch (start us, length us, event | category | flops | bytes accessed | tf_op | source)
XLA Modules:
  0.0 37.2 jit_solution(17230360629635714284)
XLA Ops:
  0.6 35.0 %jacobi_sweeps.1 = (f32[5,8,16,512]{3,2,1,0:T(8,128)S(1)}, f32[8,128]{1,0:T(8,128)S(1)}) custom-call(f32[5,8,16,512]{3,2,1,0:T(8,128)} %start_ref.1, f32[5,8,16,512]{3,2,1,0:T(8,128)} %source_ref.1, f32[5,8,16,512]{3,2,1,0:T(8,128)} %flow_ref.1, f32[5,5,8,16,512]{4,3,2,1,0:T(8,128)} %precond_ref.1, f32[5,3,5]{2,1,0:T(4,128)} %bitcast.1, s32[8,16]{1,0:T(8,128)} %codes_ref.1), custom_call_target="tpu_custom_call" | custom-call | flops 40000000 | bytes 13000000 | tf_op jit(solution)/shard_map/jacobi_sweeps/pallas_call | solution.py:418
  35.7 1.6 %deliver.1 = (f32[5,8,16,512]{3,2,1,0:T(8,128)}, f32[2]{0:T(128)}) custom-call(f32[5,8,16,512]{3,2,1,0:T(8,128)S(1)} %get-tuple-element.4.adjoint_vmem, f32[8,128]{1,0:T(8,128)S(1)} %get-tuple-element.5.sums_ref), custom_call_target="tpu_custom_call" | custom-call | tf_op jit(solution)/shard_map/deliver/pallas_call | solution.py:460

commit v3 on v2

--- a/solution.py
+++ b/solution.py
@@ -52,9 +52,6 @@
         @pl.when(there)
         def _():
             pl.semaphore_signal(barrier, inc=1, device_id=device, device_id_type=MESH)
-
-    for device in stages[0] + stages[1]:
-        pl.semaphore_signal(barrier, inc=1, device_id=device, device_id_type=MESH)
 
     load_flow = pltpu.make_async_copy(flow_ref, flow, load_sem.at[0])
     load_start = [
@@ -69,8 +66,11 @@
     ]
     load_jac = pltpu.make_async_copy(jac_ref, jac, load_sem.at[2 + chunks + NV])
     load_codes = pltpu.make_async_copy(codes_ref, codes, load_sem.at[3 + chunks + NV])
-    for copy in [load_codes, load_jac, load_flow, *load_start, load_source, *load_precond]:
+    for copy in [load_flow, *load_start, load_codes, load_jac, load_source, *load_precond]:
         copy.start()
+
+    for device in stages[0] + stages[1]:
+        pl.semaphore_signal(barrier, inc=1, device_id=device, device_id_type=MESH)
 
     def remote(src, dst, send_sem, recv_sem, device):
         return pltpu.make_async_remote_copy(
@@ -119,6 +119,37 @@
     def sent(make, side):
         make(side).wait_send()
 
+    load_flow.wait()
+
+    def speeds(i):
+        density = flow[0, i]
+        momentum = flow[1, i] * flow[1, i] + flow[2, i] * flow[2, i] + flow[3, i] * flow[3, i]
+        quarter = 0.25 * (jnp.sqrt(momentum) / density + jnp.sqrt(1.4 * flow[4, i] / density))
+        for c in range(chunks):
+            speed[i + 1, c, rows, :] = quarter[:, 128 * c : 128 * c + 128]
+
+    def loop_speeds(first, count, stride):
+        def step(t, carry):
+            speeds(first + stride * t)
+            return carry
+
+        lax.fori_loop(0, count, step, 0)
+
+    loop_speeds(0, ni, 1)
+    for copy in load_start:
+        copy.wait()
+
+    peers = sum(len(stage) for stage in stages)
+    for there, _ in i_side + j_side:
+        peers = peers + jnp.where(there, 1, 0)
+    pl.semaphore_wait(barrier, peers)
+
+    on_sides(j_side, lambda side: halo_j(0, 0, side, 0, ni), start)
+    on_sides(j_side, functools.partial(halo_speed, 1), start)
+    on_sides(i_side, functools.partial(halo_speed, 0), start)
+    for c in range(chunks):
+        on_sides(i_side, lambda side: halo_i(0, side, c, 1), start)
+
     zero_plane = jnp.zeros((chunks, nj, 128), jnp.float32)
     zero_row = jnp.zeros((1, 128), jnp.float32)
     for plane in (0, ni + 1):
@@ -169,37 +200,6 @@
         column = jnp.broadcast_to(column, (nj, 128))
         ghost[i] = jnp.where(column == 1.0, 0.0, -1.0)
         flip[i] = jnp.where((column == 0.0) & (lane == 0), 2.0, 0.0)
-
-    load_flow.wait()
-
-    def speeds(i):
-        density = flow[0, i]
-        momentum = flow[1, i] * flow[1, i] + flow[2, i] * flow[2, i] + flow[3, i] * flow[3, i]
-        quarter = 0.25 * (jnp.sqrt(momentum) / density + jnp.sqrt(1.4 * flow[4, i] / density))
-        for c in range(chunks):
-            speed[i + 1, c, rows, :] = quarter[:, 128 * c : 128 * c + 128]
-
-    def loop_speeds(first, count, stride):
-        def step(t, carry):
-            speeds(first + stride * t)
-            return carry
-
-        lax.fori_loop(0, count, step, 0)
-
-    loop_speeds(0, ni, 1)
-    for copy in load_start:
-        copy.wait()
-
-    peers = sum(len(stage) for stage in stages)
-    for there, _ in i_side + j_side:
-        peers = peers + jnp.where(there, 1, 0)
-    pl.semaphore_wait(barrier, peers)
-
-    on_sides(j_side, lambda side: halo_j(0, 0, side, 0, ni), start)
-    on_sides(j_side, functools.partial(halo_speed, 1), start)
-    on_sides(i_side, functools.partial(halo_speed, 0), start)
-    for c in range(chunks):
-        on_sides(i_side, lambda side: halo_i(0, side, c, 1), start)
 
     load_jac.wait()
     half = [[[0.5 * jac[u, d, v] for v in range(NV)] for u in range(NV)] for d in range(3)]
@@ -303,13 +303,13 @@
 
         lax.fori_loop(0, ni, step, 0)
 
-    def inner_planes(act, squares):
+    def inner_planes(act, squares, first, end):
         def step(i, carry):
             for c in range(chunks):
                 carry = act(i, c, None, carry)
             return carry
 
-        return lax.fori_loop(1, ni - 1, step, squares)
+        return lax.fori_loop(first, end, step, squares)
 
     def outer_planes(act, h, squares):
         def step(side, carry):
@@ -321,6 +321,8 @@
 
     none = jnp.zeros((nj, 128), jnp.float32)
     halves = tuple(range(chunks // 2))
+
+    outer_j = [lambda side: halo_j(1, 2, side, 0, 1), lambda side: halo_j(1, 3, side, ni - 1, 1)]
 
     load_source.wait()
     all_inside(v0)
@@ -328,22 +330,27 @@
         copy.wait()
     on_sides(j_side, functools.partial(halo_speed, 1), arrived)
     on_sides(j_side, lambda side: halo_j(0, 0, side, 0, ni), arrived)
-    squares0 = inner_planes(first_sweep, none)
-    inner_j = lambda side: halo_j(1, 1, side, 1, ni - 2)
-    on_sides(j_side, inner_j, start)
+    low = ni // 2 - 1
+    inner_j = [lambda side: halo_j(1, 1, side, 1, low), lambda side: halo_j(1, 4, side, 1 + low, ni - 2 - low)]
+    squares0 = inner_planes(first_sweep, none, 1, 1 + low)
+    on_sides(j_side, inner_j[0], start)
+    squares0 = inner_planes(first_sweep, squares0, 1 + low, ni - 1)
+    on_sides(j_side, inner_j[1], start)
     on_sides(i_side, functools.partial(halo_speed, 0), arrived)
     for h in halves:
         for c in (2 * h, 2 * h + 1):
             on_sides(i_side, lambda side: halo_i(0, side, c, 1), arrived)
         squares0 = outer_planes(first_sweep, h, squares0)
+        if h == halves[-1]:
+            for make in outer_j:
+                on_sides(j_side, make, start)
         on_sides(i_side, lambda side: halo_i(1, side, 2 * h, 2), start)
-    outer_j = [lambda side: halo_j(1, 2, side, 0, 1), lambda side: halo_j(1, 3, side, ni - 1, 1)]
-    for make in outer_j:
-        on_sides(j_side, make, start)
 
     all_inside(v1)
-    on_sides(j_side, inner_j, arrived)
-    squares1 = inner_planes(second_sweep, none)
+    squares1 = none
+    for make, first, end in zip(inner_j, (1, 1 + low), (1 + low, ni - 1)):
+        on_sides(j_side, make, arrived)
+        squares1 = inner_planes(second_sweep, squares1, first, end)
     for make in outer_j:
         on_sides(j_side, make, arrived)
     for h in halves:
@@ -392,7 +399,7 @@
     for h in halves:
         on_sides(i_side, lambda side: halo_i(1, side, 2 * h, 2), sent)
     on_sides(j_side, lambda side: halo_j(0, 0, side, 0, ni), sent)
-    for make in [inner_j, *outer_j]:
+    for make in [*inner_j, *outer_j]:
         on_sides(j_side, make, sent)
     on_sides(i_side, functools.partial(halo_speed, 0), sent)
     on_sides(j_side, functools.partial(halo_speed, 1), sent)
@@ -444,8 +451,8 @@
             dma((16,)),
             dma((2, 2, nk // 128)),
             dma((2, 2, nk // 128)),
-            dma((4, 2)),
-            dma((4, 2)),
+            dma((5, 2)),
+            dma((5, 2)),
             dma((2, 2)),
             dma((2, 2)),
             dma((30,)),

time: 37.3 us -> 37.4 us (level)
  no operation moved by 1% of the time
where the time goes in v3:
time: 37.4 us; the launch traced here: 37.3 us
  Pallas kernels  36.7 us (98%)
  between operations  0.64 us (2%)
    pallas_call x1, Pallas kernels, per_device(): pl.pallas_call(kernel, out_shape=(pltpu.VMEM(adjoint_start.shape, jnp.flo...  35.1 us
    pallas_call x1, Pallas kernels, per_device(): pl.pallas_call(functools.partial(deliver, cells_all), out_shape=(jax.Shap...  1.58 us

profile of v3, /device:TPU:1, one launch (start us, length us, event | category | flops | bytes accessed | tf_op | source)
XLA Modules:
  0.0 37.3 jit_solution(5507441404809794858)
XLA Ops:
  0.6 35.1 %jacobi_sweeps.1 = (f32[5,8,16,512]{3,2,1,0:T(8,128)S(1)}, f32[8,128]{1,0:T(8,128)S(1)}) custom-call(f32[5,8,16,512]{3,2,1,0:T(8,128)} %start_ref.1, f32[5,8,16,512]{3,2,1,0:T(8,128)} %source_ref.1, f32[5,8,16,512]{3,2,1,0:T(8,128)} %flow_ref.1, f32[5,5,8,16,512]{4,3,2,1,0:T(8,128)} %precond_ref.1, f32[5,3,5]{2,1,0:T(4,128)} %bitcast.1, s32[8,16]{1,0:T(8,128)} %codes_ref.1), custom_call_target="tpu_custom_call" | custom-call | flops 40000000 | bytes 13000000 | tf_op jit(solution)/shard_map/jacobi_sweeps/pallas_call | solution.py:425
  35.7 1.6 %deliver.1 = (f32[5,8,16,512]{3,2,1,0:T(8,128)}, f32[2]{0:T(128)}) custom-call(f32[5,8,16,512]{3,2,1,0:T(8,128)S(1)} %get-tuple-element.4.adjoint_vmem, f32[8,128]{1,0:T(8,128)S(1)} %get-tuple-element.5.sums_ref), custom_call_target="tpu_custom_call" | custom-call | tf_op jit(solution)/shard_map/deliver/pallas_call | solution.py:467
